TPU v7x, 32 devices: a whole 2x2x4 slice. The times are simulated.
32 devices in a mesh: tile: 16 (over z, y, x), rep: 2 (over core).
Axes of the slice: x: 2, y: 2, z: 4, core: 2. Of those that a mesh axis runs over, the one named last changes fastest.
Arguments:
- fields: bfloat16 [2, 16, 16, 16, 256], P('rep', 'tile'), may hold values from -6 to 6
- upstream: bfloat16 [2, 16, 16, 16, 256], P('rep', 'tile'), may hold values from -6 to 6
- kernel: float32 [7, 7, 256], replicated, may hold values from -0.875 to 0.875
- gain: float32 [256], replicated, may hold values from 0.1 to 1.9
- w_up: bfloat16 [256, 1024], replicated, may hold values from -0.375 to 0.375
- w_down: bfloat16 [1024, 256], replicated, may hold values from -0.1875 to 0.1875
- scale: float32 [256], replicated, may hold values from 0.1 to 1
- spins: int32 [16], replicated, may hold values from 0 to 3
- corner_counts: int32 [16, 4], replicated, may hold values 0 or 1
Outputs:
- field_grad: bfloat16 [2, 16, 16, 16, 256], P('rep', 'tile')
- kernel_grad: float32 [7, 7, 256], replicated
- gain_grad: float32 [256], replicated
- up_grad: float32 [256, 1024], replicated
- down_grad: float32 [1024, 256], replicated
- scale_grad: float32 [256], replicated
All inputs are finite; a program needn't handle non-finite values.
Results may differ from a plain program's by a relative error of at most 0.0067.
Values may be sent and summed in bfloat16 or wider, within the bound.
A program may use at most 64 MiB of HBM per device.

v0:
```python
import math

import jax
import jax.numpy as jnp
from jax import lax
from jax.sharding import PartitionSpec as P

epsilon = 1e-06
gelu_scale = 0.7978845608028654
gelu_cubic = 0.044715


def for_sending(array):

    def short(part):
        return part.astype(jnp.bfloat16) if part.dtype == jnp.float32 else part

    return jax.tree.map(short, array)


def shifted(block, axis, distance):
    devices = range(lax.axis_size(axis))
    route = [((i - distance) % len(devices), i) for i in devices]
    return lax.ppermute(block, axis, route)


def rotate(field, quarter):
    return jnp.rot90(field, quarter, axes=(-3, -2))


def edge_strips(field):
    return jnp.stack([rotate(field, side_idx)[..., :3, :, :] for side_idx in range(4)], axis=-4)


def corner_blocks(field):
    return jnp.stack([rotate(field, side_idx)[..., :3, :3, :] for side_idx in range(4)], axis=-4)


def assemble(field, halo_cells, corner_cells):
    widths = [(0, 0)] * (field.ndim - 3) + [(3, 3), (3, 3), (0, 0)]
    padded = jnp.pad(field, widths)
    for side_idx in range(4):
        turned = rotate(padded, side_idx)
        turned = turned.at[..., :3, 3:-3, :].set(halo_cells[..., side_idx, ::-1, :, :])
        turned = turned.at[..., :3, :3, :].set(corner_cells[..., side_idx, ::-1, ::-1, :])
        padded = rotate(turned, -side_idx)
    return padded


def split_padded(grad_pad):
    halo_parts = []
    corner_parts = []
    for side_idx in range(4):
        turned = rotate(grad_pad, side_idx)
        halo_parts.append(turned[..., 2::-1, 3:-3, :])
        corner_parts.append(turned[..., 2::-1, 2::-1, :])
    return (
        grad_pad[..., 3:-3, 3:-3, :],
        jnp.stack(halo_parts, axis=-4),
        jnp.stack(corner_parts, axis=-4),
    )


def strips_back(strip_grads, corner_grads, shape):
    summed = jnp.zeros(shape, jnp.float32)
    for side_idx in range(4):
        turned = rotate(summed, side_idx)
        turned = turned.at[..., :3, :, :].add(strip_grads[..., side_idx, :, :, :])
        turned = turned.at[..., :3, :3, :].add(corner_grads[..., side_idx, :, :, :])
        summed = rotate(turned, -side_idx)
    return summed


def block_grads(padded, upstream, kernel, gain, w_up, w_down, scale):
    side_len = upstream.shape[-2]
    channels = upstream.shape[-1]
    widened = padded.astype(jnp.float32)
    conv_sum = jnp.zeros(upstream.shape, jnp.float32)
    for row_off in range(7):
        for col_off in range(7):
            conv_sum = (
                conv_sum
                + widened[:, row_off : row_off + side_len, col_off : col_off + side_len, :]
                * kernel[row_off, col_off]
            )
    chan_mean = jnp.mean(conv_sum, axis=-1, keepdims=True)
    centred = conv_sum - chan_mean
    inv_std = lax.rsqrt(jnp.mean(centred * centred, axis=-1, keepdims=True) + epsilon)
    whitened = centred * inv_std
    normed = (whitened * gain).astype(jnp.bfloat16).reshape(-1, channels)
    hidden = jnp.dot(normed, w_up, preferred_element_type=jnp.float32)
    tangent = jnp.tanh(gelu_scale * (hidden + gelu_cubic * hidden * hidden * hidden))
    activated = (0.5 * hidden * (1.0 + tangent)).astype(jnp.bfloat16)
    projected = jnp.dot(activated, w_down, preferred_element_type=jnp.float32)
    upstream_flat = upstream.reshape(-1, channels).astype(jnp.float32)
    g_scale = jnp.sum(upstream_flat * projected, axis=0)
    d_out = (upstream_flat * scale).astype(jnp.bfloat16)
    contract_rows = (((0,), (0,)), ((), ()))
    contract_cols = (((1,), (1,)), ((), ()))
    g_down = lax.dot_general(activated, d_out, contract_rows, preferred_element_type=jnp.float32)
    d_act = lax.dot_general(d_out, w_down, contract_cols, preferred_element_type=jnp.float32)
    gelu_slope = 0.5 * (1.0 + tangent) + 0.5 * hidden * (1.0 - tangent * tangent) * gelu_scale * (
        1.0 + 3.0 * gelu_cubic * hidden * hidden
    )
    d_hidden = (d_act * gelu_slope).astype(jnp.bfloat16)
    g_up = lax.dot_general(normed, d_hidden, contract_rows, preferred_element_type=jnp.float32)
    d_normed = lax.dot_general(
        d_hidden, w_up, contract_cols, preferred_element_type=jnp.float32
    ).reshape(conv_sum.shape)
    g_gain = jnp.sum(d_normed * whitened, axis=(0, 1, 2))
    d_white = d_normed * gain
    d_conv = inv_std * (
        d_white
        - jnp.mean(d_white, axis=-1, keepdims=True)
        - whitened * jnp.mean(d_white * whitened, axis=-1, keepdims=True)
    )
    kernel_rows = []
    grad_pad = jnp.zeros(widened.shape, jnp.float32)
    for row_off in range(7):
        kernel_cols = []
        for col_off in range(7):
            window = widened[:, row_off : row_off + side_len, col_off : col_off + side_len, :]
            kernel_cols.append(jnp.sum(window * d_conv, axis=(0, 1, 2)))
            grad_pad = grad_pad.at[
                :, row_off : row_off + side_len, col_off : col_off + side_len, :
            ].add(d_conv * kernel[row_off, col_off])
        kernel_rows.append(jnp.stack(kernel_cols))
    g_kernel = jnp.stack(kernel_rows)
    return (grad_pad, (g_kernel, g_gain, g_up, g_down, g_scale))


def turn_sides(pieces, amount):
    doubled = jnp.concatenate([pieces, pieces], axis=1)
    return lax.dynamic_slice_in_dim(doubled, amount, 4, 1)


def trade_pieces(edges, corners, stride):
    edge_got = [None, None, None, None]
    corner_got = [None, None, None, None]
    edge_steps = [-stride, 1, stride, -1]
    corner_steps = [-stride - 1, -stride + 1, stride + 1, stride - 1]
    for side_idx in range(4):
        arrived = shifted(for_sending(edges[:, side_idx]), "tile", edge_steps[side_idx])
        edge_got[(side_idx + 2) % 4] = arrived
    for side_idx in range(4):
        arrived = shifted(for_sending(corners[:, side_idx]), "tile", corner_steps[side_idx])
        corner_got[(side_idx + 2) % 4] = arrived
    return (jnp.stack(edge_got, axis=1), jnp.stack(corner_got, axis=1))


def on_device(fields, upstream, kernel, gain, w_up, w_down, scale, spins, corner_counts):
    tile_count = lax.axis_size("tile")
    stride = tile_count // 2 ** ((tile_count.bit_length() - 1) // 2)
    own_tile = lax.axis_index("tile")
    own_field = fields[:, 0]
    own_upstream = upstream[:, 0]
    tile_ids = jnp.arange(tile_count, dtype=jnp.int32)
    is_mine = tile_ids == own_tile
    own_spin = jnp.sum(jnp.where(is_mine, spins, 0))
    own_counts = jnp.sum(jnp.where(is_mine[:, None], corner_counts, 0), axis=0)
    corner_keep = own_counts.astype(jnp.bfloat16)[None, :, None, None, None]
    back_turn = (4 - own_spin) % 4
    strips = edge_strips(own_field)
    blocks = corner_blocks(own_field)
    edge_got, corner_got = trade_pieces(
        turn_sides(strips, back_turn), turn_sides(blocks, back_turn), stride
    )
    halo_cells = turn_sides(edge_got, own_spin)
    corner_cells = turn_sides(corner_got, own_spin) * corner_keep
    padded = assemble(own_field, halo_cells[..., ::-1, :], corner_cells)
    grad_pad, gradients = block_grads(padded, own_upstream, kernel, gain, w_up, w_down, scale)
    interior, grad_halo, grad_corner = split_padded(grad_pad)
    halo_round = grad_halo.astype(jnp.bfloat16)
    corner_round = grad_corner.astype(jnp.bfloat16) * corner_keep
    edge_home, corner_home = trade_pieces(
        turn_sides(halo_round, back_turn), turn_sides(corner_round, back_turn), stride
    )
    strip_grads = turn_sides(edge_home, own_spin).astype(jnp.float32)[..., ::-1, :]
    corner_grads = turn_sides(corner_home, own_spin).astype(jnp.float32)
    field_grad = (
        own_upstream.astype(jnp.float32)
        + interior
        + strips_back(strip_grads, corner_grads, interior.shape)
    )
    g_kernel, g_gain, g_up, g_down, g_scale = gradients
    g_kernel, g_gain, g_up, g_down, g_scale = lax.psum(
        (g_kernel, g_gain, g_up, g_down, g_scale), ("tile", "rep")
    )
    side_len = own_field.shape[1]
    factor = 1.0 / math.sqrt(
        tile_count * lax.axis_size("rep") * own_field.shape[0] * side_len * side_len
    )
    return (
        field_grad.astype(jnp.bfloat16)[:, None],
        g_kernel * factor,
        g_gain * factor,
        g_up * factor,
        g_down * factor,
        g_scale * factor,
    )


def solution(mesh):
    return jax.shard_map(
        on_device,
        mesh=mesh,
        in_specs=(
            P("rep", "tile", None, None, None),
            P("rep", "tile", None, None, None),
            P(),
            P(),
            P(),
            P(),
            P(),
            P(),
            P(),
        ),
        out_specs=(P("rep", "tile", None, None, None), P(), P(), P(), P(), P()),
        check_vma=False,
    )
```

profile of v0, /device:TPU:1, one launch (start us, length us, event | category | flops | bytes accessed | tf_op | source)
XLA Modules:
  0.0 304.3 jit_solution(10269793642307345799)
XLA Ops:
  10.0 1.0 rev.132
  11.3 5.1 %collective-permute-start.7 = (bf16[1,3,3,256]{3,1,2,0:T(4,128)(2,1)S(1)}, bf16[1,3,3,256]{3,1,2,0:T(4,128)(2,1)S(1)}, u32[]{:S(2)}, u32[]{:S(2)}) collective-permute-start(bf16[1,3,3,256]{3,1,2,0:T(4,128)(2,1)S(1)} %get-tuple-element.921), channel_id=1, source_target_pairs={{6,0},{8,2},{10,4},{12,6},{14,8},{16,10},{18,12},{20,14},{22,16},{... | collective-permute-start | bytes 13832 | tf_op jit(solution)/shard_map/ppermute | solution.py:24
  16.6 2.2 collective-permute-start.5
  19.2 2.2 collective-permute-start.3
  24.6 0.8 and_reduce_fusion
  25.4 0.7 and_reduce_fusion.4
  29.5 3.3 %collective-permute-start.2 = (bf16[1,3,16,256]{3,1,2,0:T(4,128)(2,1)S(1)}, bf16[1,3,16,256]{3,1,2,0:T(4,128)(2,1)S(1)}, u32[]{:S(2)}, u32[]{:S(2)}) collective-permute-start(bf16[1,3,16,256]{3,1,2,0:T(4,128)(2,1)S(1)} %get-tuple-element.865), channel_id=1, source_target_pairs={{8,0},{10,2},{12,4},{14,6},{16,8},{18,10},{20,12},{22,14},{24,16},... | collective-permute-start | bytes 73736 | tf_op jit(solution)/shard_map/ppermute | solution.py:24
  32.8 1.2 collective-permute-start.1
  34.0 0.7 collective-permute-start
  35.6 3.1 %collective-permute-done = bf16[1,3,16,256]{3,1,2,0:T(4,128)(2,1)S(1)} collective-permute-done((bf16[1,3,16,256]{3,1,2,0:T(4,128)(2,1)S(1)}, bf16[1,3,16,256]{3,1,2,0:T(4,128)(2,1)S(1)}, u32[]{:S(2)}, u32[]{:S(2)}) %collective-permute-start) | collective-permute-done | bytes 24608 | tf_op jit(solution)/shard_map/ppermute | solution.py:24
  39.6 1.9 fusion.17
  41.5 1.4 scatter.26
  43.4 1.9 bitcast_select_fusion.1
  45.3 1.4 scatter.30
  46.9 1.9 bitcast_select_fusion.2
  48.8 1.4 scatter.34
  50.8 1.9 bitcast_select_fusion
  52.7 1.4 scatter.36
  54.3 1.7 fusion.29
  57.4 1.6 fusion.28
  59.0 0.8 fusion
  61.0 1.4 multiply_reduce_fusion.1
  63.0 1.2 multiply_add_fusion.1
  64.2 1.5 scatter-add.191
  65.6 2.0 add_select_fusion.4
  67.6 1.6 scatter-add.194
  69.3 1.9 add_select_fusion.3
  71.2 1.5 scatter-add.195
  72.7 2.0 add_select_fusion.2
  74.7 1.7 scatter-add.196
  76.4 1.9 add_select_fusion.1
  78.2 1.5 scatter-add.199
  79.8 2.0 add_select_fusion
  81.8 1.6 scatter-add.200
  98.2 1.0 multiply_reduce_fusion.37
  99.9 1.3 fusion.45
  101.3 1.5 fusion.1
  106.9 39.6 %all-reduce.3 = (f32[7,7,256]{2,1,0:T(8,128)S(1)}, f32[256]{0:T(256)S(1)}, f32[256]{0:T(256)S(1)}) all-reduce(f32[7,7,256]{2,1,0:T(8,128)S(1)} %constant_dynamic-update-slice_fusion.56, f32[256]{0:T(256)S(1)} %copy-done.13, f32[256]{0:T(256)S(1)} %fusion.1), channel_id=1, replica_groups=mesh['tile'=16,'rep'=2] {'tile','rep'}, use_global_device_ids=true, to_apply=%region_61.62 | all-reduce | flops 13056 | bytes 104448 | tf_op jit(solution)/shard_map/psum | solution.py:186
  149.7 4.4 %collective-permute-start.12 = (bf16[1,3,3,256]{3,1,2,0:T(4,128)(2,1)S(1)}, bf16[1,3,3,256]{3,1,2,0:T(4,128)(2,1)S(1)}, u32[]{:S(2)}, u32[]{:S(2)}) collective-permute-start(bf16[1,3,3,256]{3,1,2,0:T(4,128)(2,1)S(1)} %get-tuple-element.928), channel_id=1, source_target_pairs={{22,0},{24,2},{26,4},{28,6},{30,8},{0,10},{2,12},{4,14},{6,16},{8,... | collective-permute-start | bytes 13832 | tf_op jit(solution)/shard_map/ppermute | solution.py:24
  154.1 1.6 collective-permute-start.15
  156.6 1.8 collective-permute-start.11
  158.4 2.1 collective-permute-start.10
  161.1 1.1 collective-permute-start.9
  162.2 1.1 collective-permute-start.8
  163.5 3.5 %collective-permute-done.8 = bf16[1,3,16,256]{3,1,2,0:T(4,128)(2,1)S(1)} collective-permute-done((bf16[1,3,16,256]{3,1,2,0:T(4,128)(2,1)S(1)}, bf16[1,3,16,256]{3,1,2,0:T(4,128)(2,1)S(1)}, u32[]{:S(2)}, u32[]{:S(2)}) %collective-permute-start.8) | collective-permute-done | bytes 24608 | tf_op jit(solution)/shard_map/ppermute | solution.py:24
  170.2 123.7 %all-reduce.7.cloned.1.call-done = (f32[256,1024]{1,0:T(8,128)}, f32[1024,256]{1,0:T(8,128)}) async-done(((f32[256,1024]{1,0:T(8,128)}, f32[1024,256]{1,0:T(8,128)}), (f32[256,1024]{1,0:T(8,128)}, f32[1024,256]{1,0:T(8,128)})) %all-reduce.7.cloned.1.call-update) | async-done | bytes 2097168 | tf_op jit(solution)/shard_map/psum | solution.py:186
  293.9 2.4 broadcast_multiply_fusion.1
  296.3 1.1 broadcast_multiply_fusion
  (368 shorter events, 39.7 us)
Async XLA Ops:
  7.2 49.9 %copy-start = (bf16[256,1024]{1,0:T(8,128)(2,1)S(1)}, bf16[256,1024]{1,0:T(8,128)(2,1)}, u32[]{:S(2)}) copy-start(bf16[256,1024]{1,0:T(8,128)(2,1)} %param.143) | copy-start | bytes 1572868
  7.2 286.7 %all-reduce.7.cloned.1.call-start = ((), (), s32[]{:S(2)}) async-start(), calls=%async_computation | async-start | bytes 4194304 | tf_op jit(solution)/shard_map/psum | solution.py:186
  7.2 0.7 copy-start.39
  10.0 1.0 copy-start.1
  11.3 23.5 %collective-permute-start.7 = (bf16[1,3,3,256]{3,1,2,0:T(4,128)(2,1)S(1)}, bf16[1,3,3,256]{3,1,2,0:T(4,128)(2,1)S(1)}, u32[]{:S(2)}, u32[]{:S(2)}) collective-permute-start(bf16[1,3,3,256]{3,1,2,0:T(4,128)(2,1)S(1)} %get-tuple-element.921), channel_id=1, source_target_pairs={{6,0},{8,2},{10,4},{12,6},{14,8},{16,10},{18,12},{20,14},{22,16},{... | collective-permute-start | bytes 13832 | tf_op jit(solution)/shard_map/ppermute | solution.py:24
  16.4 17.6 %collective-permute-start.6 = (bf16[1,3,3,256]{3,1,2,0:T(4,128)(2,1)S(1)}, bf16[1,3,3,256]{3,1,2,0:T(4,128)(2,1)S(1)}, u32[]{:S(2)}, u32[]{:S(2)}) collective-permute-start(bf16[1,3,3,256]{3,1,2,0:T(4,128)(2,1)S(1)} %get-tuple-element.922), channel_id=1, source_target_pairs={{10,0},{12,2},{14,4},{16,6},{18,8},{20,10},{22,12},{24,14},{26,16}... | collective-permute-start | bytes 13832 | tf_op jit(solution)/shard_map/ppermute | solution.py:24
  16.6 16.2 %collective-permute-start.5 = (bf16[1,3,3,256]{3,1,2,0:T(4,128)(2,1)S(1)}, bf16[1,3,3,256]{3,1,2,0:T(4,128)(2,1)S(1)}, u32[]{:S(2)}, u32[]{:S(2)}) collective-permute-start(bf16[1,3,3,256]{3,1,2,0:T(4,128)(2,1)S(1)} %get-tuple-element.923), channel_id=1, source_target_pairs={{26,0},{28,2},{30,4},{0,6},{2,8},{4,10},{6,12},{8,14},{10,16},{12,... | collective-permute-start | bytes 13832 | tf_op jit(solution)/shard_map/ppermute | solution.py:24
  18.7 10.8 %collective-permute-start.4 = (bf16[1,3,3,256]{3,1,2,0:T(4,128)(2,1)S(1)}, bf16[1,3,3,256]{3,1,2,0:T(4,128)(2,1)S(1)}, u32[]{:S(2)}, u32[]{:S(2)}) collective-permute-start(bf16[1,3,3,256]{3,1,2,0:T(4,128)(2,1)S(1)} %get-tuple-element.924), channel_id=1, source_target_pairs={{22,0},{24,2},{26,4},{28,6},{30,8},{0,10},{2,12},{4,14},{6,16},{8,... | collective-permute-start | bytes 13832 | tf_op jit(solution)/shard_map/ppermute | solution.py:24
  19.1 2.3 copy-start.6
  19.1 5.5 %copy-start.34 = (s32[4]{0:T(128)S(1)}, s32[4]{0:T(128)}, u32[]{:S(2)}) copy-start(s32[4]{0:T(128)} %constant.1857.clone.1) | copy-start | bytes 52
  19.1 6.3 %copy-start.37 = (s32[4]{0:T(128)S(1)}, s32[4]{0:T(128)}, u32[]{:S(2)}) copy-start(s32[4]{0:T(128)} %constant.1842.clone.1) | copy-start | bytes 52
  19.2 7.1 %copy-start.5 = (bf16[1,1,16,16,256]{4,3,2,1,0:T(8,128)(2,1)S(1)}, bf16[1,1,16,16,256]{4,3,2,1,0:T(8,128)(2,1)}, u32[]{:S(2)}) copy-start(bf16[1,1,16,16,256]{4,3,2,1,0:T(8,128)(2,1)} %param.140) | copy-start | bytes 393220
  19.2 19.6 %collective-permute-start.3 = (bf16[1,3,16,256]{3,1,2,0:T(4,128)(2,1)S(1)}, bf16[1,3,16,256]{3,1,2,0:T(4,128)(2,1)S(1)}, u32[]{:S(2)}, u32[]{:S(2)}) collective-permute-start(bf16[1,3,16,256]{3,1,2,0:T(4,128)(2,1)S(1)} %get-tuple-element.864), channel_id=1, source_target_pairs={{30,0},{0,2},{2,4},{4,6},{6,8},{8,10},{10,12},{12,14},{14,16},{16,... | collective-permute-start | bytes 73736 | tf_op jit(solution)/shard_map/ppermute | solution.py:24
  25.4 0.7 copy-start.35
  29.4 5.4 %copy-start.32 = (bf16[4]{0:T(256)(128)(2,1)}, bf16[4]{0:T(256)(128)(2,1)S(1)}, u32[]{:S(2)}) copy-start(bf16[4]{0:T(256)(128)(2,1)S(1)} %convert_element_type.76) | copy-start | bytes 28
  29.5 9.3 %collective-permute-start.2 = (bf16[1,3,16,256]{3,1,2,0:T(4,128)(2,1)S(1)}, bf16[1,3,16,256]{3,1,2,0:T(4,128)(2,1)S(1)}, u32[]{:S(2)}, u32[]{:S(2)}) collective-permute-start(bf16[1,3,16,256]{3,1,2,0:T(4,128)(2,1)S(1)} %get-tuple-element.865), channel_id=1, source_target_pairs={{8,0},{10,2},{12,4},{14,6},{16,8},{18,10},{20,12},{22,14},{24,16},... | collective-permute-start | bytes 73736 | tf_op jit(solution)/shard_map/ppermute | solution.py:24
  32.8 6.0 %collective-permute-start.1 = (bf16[1,3,16,256]{3,1,2,0:T(4,128)(2,1)S(1)}, bf16[1,3,16,256]{3,1,2,0:T(4,128)(2,1)S(1)}, u32[]{:S(2)}, u32[]{:S(2)}) collective-permute-start(bf16[1,3,16,256]{3,1,2,0:T(4,128)(2,1)S(1)} %get-tuple-element.866), channel_id=1, source_target_pairs={{2,0},{4,2},{6,4},{8,6},{10,8},{12,10},{14,12},{16,14},{18,16},{20... | collective-permute-start | bytes 73736 | tf_op jit(solution)/shard_map/ppermute | solution.py:24
  34.0 4.7 %collective-permute-start = (bf16[1,3,16,256]{3,1,2,0:T(4,128)(2,1)S(1)}, bf16[1,3,16,256]{3,1,2,0:T(4,128)(2,1)S(1)}, u32[]{:S(2)}, u32[]{:S(2)}) collective-permute-start(bf16[1,3,16,256]{3,1,2,0:T(4,128)(2,1)S(1)} %get-tuple-element.867), channel_id=1, source_target_pairs={{24,0},{26,2},{28,4},{30,6},{0,8},{2,10},{4,12},{6,14},{8,16},{10,... | collective-permute-start | bytes 73736 | tf_op jit(solution)/shard_map/ppermute | solution.py:24
  56.3 0.7 copy-start.7
  57.4 1.6 copy-start.3
  57.4 1.6 copy-start.38
  99.9 1.3 copy-start.4
  101.2 2.9 copy-start.29
  101.2 2.9 copy-start.30
  101.2 3.0 copy-start.31
  101.2 3.6 %copy-start.22 = (f32[256]{0:T(256)S(1)}, f32[256]{0:T(256)}, u32[]{:S(2)}) copy-start(f32[256]{0:T(256)} %get-tuple-element.794) | copy-start | bytes 3076
  101.2 3.6 %copy-start.23 = (f32[256]{0:T(256)S(1)}, f32[256]{0:T(256)}, u32[]{:S(2)}) copy-start(f32[256]{0:T(256)} %get-tuple-element.795) | copy-start | bytes 3076
  101.2 3.6 %copy-start.24 = (f32[256]{0:T(256)S(1)}, f32[256]{0:T(256)}, u32[]{:S(2)}) copy-start(f32[256]{0:T(256)} %get-tuple-element.796) | copy-start | bytes 3076
  101.3 3.6 %copy-start.25 = (f32[256]{0:T(256)S(1)}, f32[256]{0:T(256)}, u32[]{:S(2)}) copy-start(f32[256]{0:T(256)} %get-tuple-element.797) | copy-start | bytes 3076
  101.3 3.6 %copy-start.26 = (f32[256]{0:T(256)S(1)}, f32[256]{0:T(256)}, u32[]{:S(2)}) copy-start(f32[256]{0:T(256)} %get-tuple-element.798) | copy-start | bytes 3076
  101.3 3.6 %copy-start.27 = (f32[256]{0:T(256)S(1)}, f32[256]{0:T(256)}, u32[]{:S(2)}) copy-start(f32[256]{0:T(256)} %get-tuple-element.799) | copy-start | bytes 3076
  101.3 4.3 %copy-start.15 = (f32[256]{0:T(256)S(1)}, f32[256]{0:T(256)}, u32[]{:S(2)}) copy-start(f32[256]{0:T(256)} %get-tuple-element.787) | copy-start | bytes 3076
  101.3 4.3 %copy-start.16 = (f32[256]{0:T(256)S(1)}, f32[256]{0:T(256)}, u32[]{:S(2)}) copy-start(f32[256]{0:T(256)} %get-tuple-element.788) | copy-start | bytes 3076
  101.3 4.3 %copy-start.17 = (f32[256]{0:T(256)S(1)}, f32[256]{0:T(256)}, u32[]{:S(2)}) copy-start(f32[256]{0:T(256)} %get-tuple-element.789) | copy-start | bytes 3076
  101.3 4.3 %copy-start.18 = (f32[256]{0:T(256)S(1)}, f32[256]{0:T(256)}, u32[]{:S(2)}) copy-start(f32[256]{0:T(256)} %get-tuple-element.790) | copy-start | bytes 3076
  101.3 4.3 %copy-start.19 = (f32[256]{0:T(256)S(1)}, f32[256]{0:T(256)}, u32[]{:S(2)}) copy-start(f32[256]{0:T(256)} %get-tuple-element.791) | copy-start | bytes 3076
  101.3 4.3 %copy-start.20 = (f32[256]{0:T(256)S(1)}, f32[256]{0:T(256)}, u32[]{:S(2)}) copy-start(f32[256]{0:T(256)} %get-tuple-element.792) | copy-start | bytes 3076
  103.3 0.7 copy-start.8
  106.3 0.7 copy-start.13
  149.7 8.8 %collective-permute-start.12 = (bf16[1,3,3,256]{3,1,2,0:T(4,128)(2,1)S(1)}, bf16[1,3,3,256]{3,1,2,0:T(4,128)(2,1)S(1)}, u32[]{:S(2)}, u32[]{:S(2)}) collective-permute-start(bf16[1,3,3,256]{3,1,2,0:T(4,128)(2,1)S(1)} %get-tuple-element.928), channel_id=1, source_target_pairs={{22,0},{24,2},{26,4},{28,6},{30,8},{0,10},{2,12},{4,14},{6,16},{8,... | collective-permute-start | bytes 13832 | tf_op jit(solution)/shard_map/ppermute | solution.py:24
  154.1 9.3 %collective-permute-start.15 = (bf16[1,3,3,256]{3,1,2,0:T(4,128)(2,1)S(1)}, bf16[1,3,3,256]{3,1,2,0:T(4,128)(2,1)S(1)}, u32[]{:S(2)}, u32[]{:S(2)}) collective-permute-start(bf16[1,3,3,256]{3,1,2,0:T(4,128)(2,1)S(1)} %get-tuple-element.925), channel_id=1, source_target_pairs={{6,0},{8,2},{10,4},{12,6},{14,8},{16,10},{18,12},{20,14},{22,16},{... | collective-permute-start | bytes 13832 | tf_op jit(solution)/shard_map/ppermute | solution.py:24
  155.8 6.5 %collective-permute-start.14 = (bf16[1,3,3,256]{3,1,2,0:T(4,128)(2,1)S(1)}, bf16[1,3,3,256]{3,1,2,0:T(4,128)(2,1)S(1)}, u32[]{:S(2)}, u32[]{:S(2)}) collective-permute-start(bf16[1,3,3,256]{3,1,2,0:T(4,128)(2,1)S(1)} %get-tuple-element.926), channel_id=1, source_target_pairs={{10,0},{12,2},{14,4},{16,6},{18,8},{20,10},{22,12},{24,14},{26,16}... | collective-permute-start | bytes 13832 | tf_op jit(solution)/shard_map/ppermute | solution.py:24
  155.9 5.2 %collective-permute-start.13 = (bf16[1,3,3,256]{3,1,2,0:T(4,128)(2,1)S(1)}, bf16[1,3,3,256]{3,1,2,0:T(4,128)(2,1)S(1)}, u32[]{:S(2)}, u32[]{:S(2)}) collective-permute-start(bf16[1,3,3,256]{3,1,2,0:T(4,128)(2,1)S(1)} %get-tuple-element.927), channel_id=1, source_target_pairs={{26,0},{28,2},{30,4},{0,6},{2,8},{4,10},{6,12},{8,14},{10,16},{12,... | collective-permute-start | bytes 13832 | tf_op jit(solution)/shard_map/ppermute | solution.py:24
  156.6 10.5 %collective-permute-start.11 = (bf16[1,3,16,256]{3,1,2,0:T(4,128)(2,1)S(1)}, bf16[1,3,16,256]{3,1,2,0:T(4,128)(2,1)S(1)}, u32[]{:S(2)}, u32[]{:S(2)}) collective-permute-start(bf16[1,3,16,256]{3,1,2,0:T(4,128)(2,1)S(1)} %get-tuple-element.856), channel_id=1, source_target_pairs={{30,0},{0,2},{2,4},{4,6},{6,8},{8,10},{10,12},{12,14},{14,16},{16,... | collective-permute-start | bytes 73736 | tf_op jit(solution)/shard_map/ppermute | solution.py:24
  158.4 8.7 %collective-permute-start.10 = (bf16[1,3,16,256]{3,1,2,0:T(4,128)(2,1)S(1)}, bf16[1,3,16,256]{3,1,2,0:T(4,128)(2,1)S(1)}, u32[]{:S(2)}, u32[]{:S(2)}) collective-permute-start(bf16[1,3,16,256]{3,1,2,0:T(4,128)(2,1)S(1)} %get-tuple-element.857), channel_id=1, source_target_pairs={{8,0},{10,2},{12,4},{14,6},{16,8},{18,10},{20,12},{22,14},{24,16},... | collective-permute-start | bytes 73736 | tf_op jit(solution)/shard_map/ppermute | solution.py:24
  161.1 5.9 %collective-permute-start.9 = (bf16[1,3,16,256]{3,1,2,0:T(4,128)(2,1)S(1)}, bf16[1,3,16,256]{3,1,2,0:T(4,128)(2,1)S(1)}, u32[]{:S(2)}, u32[]{:S(2)}) collective-permute-start(bf16[1,3,16,256]{3,1,2,0:T(4,128)(2,1)S(1)} %get-tuple-element.858), channel_id=1, source_target_pairs={{2,0},{4,2},{6,4},{8,6},{10,8},{12,10},{14,12},{16,14},{18,16},{20... | collective-permute-start | bytes 73736 | tf_op jit(solution)/shard_map/ppermute | solution.py:24
  162.2 4.8 %collective-permute-start.8 = (bf16[1,3,16,256]{3,1,2,0:T(4,128)(2,1)S(1)}, bf16[1,3,16,256]{3,1,2,0:T(4,128)(2,1)S(1)}, u32[]{:S(2)}, u32[]{:S(2)}) collective-permute-start(bf16[1,3,16,256]{3,1,2,0:T(4,128)(2,1)S(1)} %get-tuple-element.859), channel_id=1, source_target_pairs={{24,0},{26,2},{28,4},{30,6},{0,8},{2,10},{4,12},{6,14},{8,16},{10,... | collective-permute-start | bytes 73736 | tf_op jit(solution)/shard_map/ppermute | solution.py:24
  293.9 2.4 copy-start.2
  (9 other events, 5.9 us)
Sparse Core Ops, SparseCore 0:
  158.5 135.3 all-reduce.6
where the time goes:
time: 307 us; the launch traced here: 304 us
  waiting for transfers between devices  131 us (43%)
  local copies, waits for them, and re-layouts  46 us (15%)
  blocking collectives  39.6 us (13%)
  other arithmetic  34.9 us (11%)
  starting transfers between devices  27.9 us (9%)
  between operations  18.9 us (6%)
  matrix products  5.9 us (2%)
    psum x1, waiting for transfers between devices, on_device(): lax.psum((g_kernel, g_gain, g_up, g_down, g_scale), ('tile', 'rep'))  124 us
    psum x1, blocking collectives, on_device(): lax.psum((g_kernel, g_gain, g_up, g_down, g_scale), ('tile', 'rep'))  39.6 us
    ppermute x16, starting transfers between devices, shifted(): return lax.ppermute(block, axis, route)  27.8 us
    scatter-add x43, local copies, waits for them, and re-layouts, block_grads(): grad_pad = grad_pad.at[:, row_off:row_off + side_len, col_off:col_off + s...  21.9 us
    another operation x15, other arithmetic  18.8 us
    ppermute x16, waiting for transfers between devices, shifted(): return lax.ppermute(block, axis, route)  7.36 us
    unnamed x138, local copies, waits for them, and re-layouts  6.77 us
  transfers between devices with their start and end apart: 17, of which 4 were waited for; matrix products, arithmetic and copies ran while one was open for 3% of the time, Pallas kernels for 0%

commit v1 on v0

v1 whole, which is shorter than its diff:
```python
import functools
import math

import jax
import jax.numpy as jnp
import numpy as np
from jax import lax
from jax.experimental import pallas as pl
from jax.experimental.pallas import tpu as pltpu
from jax.sharding import PartitionSpec as P

epsilon = 1e-06
gelu_scale = 0.7978845608028654
gelu_cubic = 0.044715
MESH = pl.DeviceIdType.MESH
SIDE = 16
WIDE = 22
PITCH = 24
PIECE = 64
SMALL = 64
PARTS = 2


def tables():
    cells = np.arange(SIDE * SIDE).reshape(SIDE, SIDE)
    pads = np.arange(WIDE * PITCH).reshape(WIDE, PITCH)[:, :WIDE]
    cut = np.zeros((4 * PIECE, SIDE * SIDE), np.float32)
    paste = np.zeros((WIDE * PITCH, 4 * PIECE), np.float32)
    centre = np.zeros((WIDE * PITCH, SIDE * SIDE), np.float32)
    for edge in range(4):
        turned = np.rot90(cells, edge)
        wide = np.rot90(pads, edge)
        for depth in range(3):
            for along in range(SIDE):
                cut[edge * PIECE + depth * SIDE + along, turned[depth, along]] = 1
                paste[wide[2 - depth, 3 + along], edge * PIECE + depth * SIDE + SIDE - 1 - along] = 1
            for along in range(3):
                row = edge * PIECE + 48 + depth * 3 + along
                cut[row, turned[depth, along]] = 1
                paste[wide[2 - depth, 2 - along], row] = 1
    for row in range(SIDE):
        for col in range(SIDE):
            centre[pads[row + 3, col + 3], cells[row, col]] = 1
    return [jnp.asarray(t, jnp.bfloat16) for t in (cut, cut.T, paste, paste.T, centre)]


def plan(tiles, reps, rows):
    groups = []
    if reps > 1:
        groups.append(("rep", 1, reps))
    stride = 1
    while stride < tiles:
        size = 4 if tiles // stride % 4 == 0 else 2
        groups.append(("tile", stride, size))
        stride *= size
    phases = []
    for axis, stride, size in groups:
        scatter = rows % (16 * size) == 0
        out = rows // size if scatter else rows
        phases.append((axis, stride, size, scatter, rows, out))
        rows = out
    return phases


def dot(left, right, dims=((1,), (0,))):
    return lax.dot_general(left, right, (dims, ((), ())), preferred_element_type=jnp.float32)


def body(
    tiles, phases,
    field_ref, up_ref, kern_ref, gain_ref, wup_ref, wdown_ref, scale_ref, spins_ref, counts_ref,
    cut_ref, cut_t_ref, paste_ref, paste_t_ref, centre_ref,
    grad_ref, gup_ref, gdown_ref, gsmall_ref,
    pieces, sent, got, pieces_b, sent_b, got_b, turned,
    pad_ref, shift_ref, conv_ref, dact_ref, dcp_ref, dpad_ref, gbuf, agbuf, small_ref,
    send_sem, recv_sem, *bufs,
):
    count = len(phases)
    recv_bufs = bufs[:count]
    red_bufs = bufs[count : 2 * count]
    small_bufs = bufs[2 * count : 3 * count]
    tile = lax.axis_index("tile")
    rep = lax.axis_index("rep")
    side = tiles // 2 ** ((tiles.bit_length() - 1) // 2)
    steps = [-side, 1, side, -1, -side - 1, -side + 1, side + 1, side - 1]

    def across(step):
        return {"tile": lax.rem(tile + step + tiles, tiles)}

    def place(phase):
        axis, stride, size = phases[phase][:3]
        return rep if axis == "rep" else lax.rem(tile // stride, size)

    def member(phase, ahead):
        axis, stride, size = phases[phase][:3]
        pos = place(phase)
        other = lax.rem(pos + ahead, size)
        if axis == "rep":
            return {"rep": other}, other
        return {"tile": tile + (other - pos) * stride}, other

    barrier = pltpu.get_barrier_semaphore()
    greeted = 0
    for step in steps:
        pl.semaphore_signal(barrier, inc=1, device_id=across(step), device_id_type=MESH)
        greeted += 1
    for phase in range(count):
        for ahead in range(1, phases[phase][2]):
            pl.semaphore_signal(
                barrier, inc=1, device_id=member(phase, ahead)[0], device_id_type=MESH
            )
            greeted += 1

    used = [0]
    started = []

    def push(src, dst, device):
        slot = used[0]
        used[0] += 1
        copy = pltpu.make_async_remote_copy(
            src_ref=src, dst_ref=dst, send_sem=send_sem.at[slot], recv_sem=recv_sem.at[slot],
            device_id=device, device_id_type=MESH,
        )
        copy.start()
        started.append(copy)
        return copy

    spin = spins_ref[tile]
    is_corner = lax.broadcasted_iota(jnp.int32, (PIECE, 256), 0) >= 48

    def masked(piece, edge):
        keep = jnp.where(is_corner, counts_ref[tile, edge].astype(jnp.float32), 1.0)
        return (piece.astype(jnp.float32) * keep).astype(jnp.bfloat16)

    def trade(source, out, into):
        for grid in range(4):
            out[grid] = source[lax.rem(grid - spin + 4, 4)]
        copies = []
        for grid in range(4):
            copies.append(push(out.at[grid, pl.ds(0, 48)], into.at[(grid + 2) % 4, pl.ds(0, 48)], across(steps[grid])))
        for grid in range(4):
            copies.append(push(out.at[grid, pl.ds(48, 16)], into.at[(grid + 2) % 4, pl.ds(48, 16)], across(steps[4 + grid])))
        return copies

    flying = [None] * PARTS
    reached = [0] * PARTS
    offsets = []
    offset = 0
    for phase in range(count):
        if phases[phase][3]:
            offset = offset + place(phase) * phases[phase][5]
        offsets.append(offset)

    def source_of(part, phase):
        return gbuf.at[part] if phase == 0 else red_bufs[phase - 1].at[part]

    def begin(part):
        phase = reached[part]
        size, scatter, rows, out = phases[phase][2:]
        src = source_of(part, phase)
        copies = []
        if not scatter:
            recv_bufs[phase][part, place(phase)] = src[...]
        for ahead in range(1, size):
            device, other = member(phase, ahead)
            if scatter:
                start = pl.multiple_of(other * out, 16)
                copies.append(push(src.at[pl.ds(start, out)], recv_bufs[phase].at[part, ahead - 1], device))
            else:
                copies.append(push(src, recv_bufs[phase].at[part, place(phase)], device))
        flying[part] = copies

    def finish(part):
        phase = reached[part]
        size, scatter, rows, out = phases[phase][2:]
        src = source_of(part, phase)
        for copy in flying[part]:
            copy.wait_recv()
        if scatter:
            total = src[pl.ds(pl.multiple_of(place(phase) * out, 16), out)].astype(jnp.float32)
            for slot in range(size - 1):
                total = total + recv_bufs[phase][part, slot].astype(jnp.float32)
        else:
            total = recv_bufs[phase][part, 0].astype(jnp.float32)
            for slot in range(1, size):
                total = total + recv_bufs[phase][part, slot].astype(jnp.float32)
        reached[part] += 1
        if reached[part] < count:
            red_bufs[phase][part] = total.astype(jnp.bfloat16)
        else:
            agbuf[part, pl.ds(pl.multiple_of(offsets[-1], 16), out)] = total.astype(jnp.bfloat16)

    def advance(part):
        if reached[part] < count:
            finish(part)
            if reached[part] < count:
                begin(part)

    def gather(part, phase):
        size, scatter, rows, out = phases[phase][2:]
        if not scatter:
            return []
        here = agbuf.at[part, pl.ds(pl.multiple_of(offsets[phase], 16), out)]
        return [push(here, here, member(phase, ahead)[0]) for ahead in range(1, size)]

    pieces[...] = dot(cut_ref[...], field_ref[...]).astype(jnp.bfloat16).reshape(4, PIECE, 256)
    pl.semaphore_wait(barrier, greeted)
    copies = trade(pieces, sent, got)
    upstream = up_ref[...].astype(jnp.float32)
    d_out = (upstream * scale_ref[...]).astype(jnp.bfloat16)
    for block in range(4):
        cols = pl.ds(block * 256, 256)
        dact_ref[:, cols] = dot(d_out, wdown_ref[cols, :], ((1,), (1,)))
    inner = dot(centre_ref[...], field_ref[...])
    dcp_ref[0:6] = jnp.zeros((6, SIDE, 256), jnp.float32)
    dcp_ref[WIDE : WIDE + 6] = jnp.zeros((6, SIDE, 256), jnp.float32)
    small_ref[...] = jnp.zeros((SMALL, 256), jnp.float32)
    for copy in copies:
        copy.wait_recv()
    for edge in range(4):
        turned[pl.ds(edge * PIECE, PIECE), :] = masked(got[lax.rem(edge + spin, 4)], edge)
    pad_ref[...] = (inner + dot(paste_ref[...], turned[...])).reshape(WIDE, PITCH, 256)
    for col in range(7):
        shift_ref[col] = pad_ref[:, pl.ds(col, SIDE), :]

    @pl.loop(0, SIDE // 4)
    def _(group):
        acc = [jnp.zeros((SIDE, 256), jnp.float32) for _ in range(4)]
        for col in range(7):
            for row in range(7):
                tap = kern_ref[pl.ds(row * 7 + col, 1), :]
                for line in range(4):
                    acc[line] = acc[line] + shift_ref[col, group * 4 + line + row] * tap
        for line in range(4):
            conv_ref[group * 4 + line] = acc[line]

    conv = conv_ref[...].reshape(SIDE * SIDE, 256)
    gain = gain_ref[...]
    centred = conv - jnp.mean(conv, axis=1, keepdims=True)
    inv_std = lax.rsqrt(jnp.mean(centred * centred, axis=1, keepdims=True) + epsilon)
    whitened = centred * inv_std
    normed = (whitened * gain).astype(jnp.bfloat16)
    projected = jnp.zeros((SIDE * SIDE, 256), jnp.float32)
    d_normed = jnp.zeros((SIDE * SIDE, 256), jnp.float32)
    per_part = 4 // PARTS
    for block in range(4):
        cols = pl.ds(block * 256, 256)
        part, local = block // per_part, block % per_part
        h = dot(normed, wup_ref[:, cols])
        square = h * h
        t = jnp.tanh(gelu_scale * h * (1.0 + gelu_cubic * square))
        half = 0.5 * (1.0 + t)
        activated = (h * half).astype(jnp.bfloat16)
        slope = half + 0.5 * h * (1.0 - t * t) * (gelu_scale * (1.0 + 3.0 * gelu_cubic * square))
        d_hidden = (dact_ref[:, cols] * slope).astype(jnp.bfloat16)
        gbuf[part, pl.ds(local * 512, 256)] = dot(normed, d_hidden, ((0,), (0,))).astype(jnp.bfloat16)
        gbuf[part, pl.ds(local * 512 + 256, 256)] = dot(activated, d_out, ((0,), (0,))).astype(jnp.bfloat16)
        if local == per_part - 1:
            begin(part)
        projected = projected + dot(activated, wdown_ref[cols, :])
        d_normed = d_normed + dot(d_hidden, wup_ref[:, cols], ((1,), (1,)))
    for part in range(PARTS - 1):
        advance(part)

    small_ref[49:50, :] = jnp.sum(d_normed * whitened, axis=0, keepdims=True)
    small_ref[50:51, :] = jnp.sum(upstream * projected, axis=0, keepdims=True)
    d_white = d_normed * gain
    d_conv = inv_std * (
        d_white
        - jnp.mean(d_white, axis=1, keepdims=True)
        - whitened * jnp.mean(d_white * whitened, axis=1, keepdims=True)
    )
    dcp_ref[6:WIDE] = d_conv.reshape(SIDE, SIDE, 256)
    advance(PARTS - 1)

    @pl.loop(0, WIDE // 2)
    def _(group):
        total = [jnp.zeros((PITCH, 256), jnp.float32) for _ in range(2)]
        for col in range(7):
            acc = [jnp.zeros((SIDE, 256), jnp.float32) for _ in range(2)]
            for row in range(7):
                tap = kern_ref[pl.ds(row * 7 + col, 1), :]
                for line in range(2):
                    acc[line] = acc[line] + dcp_ref[group * 2 + line + 6 - row] * tap
            for line in range(2):
                long = jnp.concatenate([acc[line], jnp.zeros((8, 256), jnp.float32)], axis=0)
                total[line] = total[line] + (pltpu.roll(long, col, 0) if col else long)
        for line in range(2):
            dpad_ref[group * 2 + line] = total[line]

    rounded = dpad_ref[...].reshape(WIDE * PITCH, 256).astype(jnp.bfloat16)
    back = dot(paste_t_ref[...], rounded).astype(jnp.bfloat16)
    for edge in range(4):
        pieces_b[edge] = masked(back[edge * PIECE : (edge + 1) * PIECE], edge)
    copies = trade(pieces_b, sent_b, got_b)
    for part in range(PARTS):
        advance(part)

    for col in range(7):
        def line_sum(line, acc, col=col):
            grads = dcp_ref[line + 6]
            return tuple(acc[row] + shift_ref[col, line + row] * grads for row in range(7))

        sums = lax.fori_loop(
            0, SIDE, line_sum, tuple(jnp.zeros((SIDE, 256), jnp.float32) for _ in range(7))
        )
        for row in range(7):
            small_ref[pl.ds(row * 7 + col, 1), :] = jnp.sum(sums[row], axis=0, keepdims=True)

    def small_begin(phase):
        own = small_bufs[phase].at[place(phase)]
        own[...] = small_ref[...].astype(jnp.bfloat16)
        return [push(own, own, member(phase, ahead)[0]) for ahead in range(1, phases[phase][2])]

    def small_finish(phase, copies):
        for copy in copies:
            copy.wait_recv()
        total = small_bufs[phase][0].astype(jnp.float32)
        for slot in range(1, phases[phase][2]):
            total = total + small_bufs[phase][slot].astype(jnp.float32)
        small_ref[...] = total

    small_copies = small_begin(count - 1)
    for _ in range(count):
        for part in range(PARTS):
            advance(part)
    gathers = [gather(part, count - 1) for part in range(PARTS)]

    for copy in copies:
        copy.wait_recv()
    for edge in range(4):
        turned[pl.ds(edge * PIECE, PIECE), :] = got_b[lax.rem(edge + spin, 4)]
    inside = dpad_ref[3 : 3 + SIDE, 3 : 3 + SIDE, :].reshape(SIDE * SIDE, 256)
    home = dot(cut_t_ref[...], turned[...])
    grad_ref[...] = (upstream + inside + home).astype(jnp.bfloat16)

    for phase in range(count - 1, -1, -1):
        small_finish(phase, small_copies)
        if phase > 0:
            small_copies = small_begin(phase - 1)
        for part in range(PARTS):
            for copy in gathers[part]:
                copy.wait_recv()
            if phase > 0:
                gathers[part] = gather(part, phase - 1)
    for block in range(4):
        part, local = block // per_part, block % per_part
        gup_ref[:, pl.ds(block * 256, 256)] = agbuf[part, pl.ds(local * 512, 256)]
        gdown_ref[pl.ds(block * 256, 256), :] = agbuf[part, pl.ds(local * 512 + 256, 256)]
    gsmall_ref[...] = small_ref[...]
    for copy in started:
        copy.wait_send()


def on_device(tiles, reps, fields, upstream, kernel, gain, w_up, w_down, scale, spins, corner_counts):
    rows = 2048 // PARTS
    phases = plan(tiles, reps, rows)
    bf16, f32 = jnp.bfloat16, jnp.float32
    per_part = sum(size - 1 for _, _, size, _, _, _ in phases)
    sems = 16 + per_part * (2 * PARTS + 1)
    piece = pltpu.VMEM((4, PIECE, 256), bf16)
    scratch = [
        piece, piece, piece, piece, piece, piece,
        pltpu.VMEM((4 * PIECE, 256), bf16),
        pltpu.VMEM((WIDE, PITCH, 256), f32),
        pltpu.VMEM((7, WIDE, SIDE, 256), f32),
        pltpu.VMEM((SIDE, SIDE, 256), f32),
        pltpu.VMEM((SIDE * SIDE, 1024), f32),
        pltpu.VMEM((WIDE + 6, SIDE, 256), f32),
        pltpu.VMEM((WIDE, PITCH, 256), f32),
        pltpu.VMEM((PARTS, rows, 256), bf16),
        pltpu.VMEM((PARTS, rows, 256), bf16),
        pltpu.VMEM((SMALL, 256), f32),
        pltpu.SemaphoreType.DMA((sems,)),
        pltpu.SemaphoreType.DMA((sems,)),
    ]
    for _, _, size, scatter, _, out in phases:
        scratch.append(pltpu.VMEM((PARTS, size - 1 if scatter else size, out, 256), bf16))
    for _, _, size, scatter, _, out in phases:
        scratch.append(pltpu.VMEM((PARTS, out, 256), bf16))
    for _, _, size, _, _, _ in phases:
        scratch.append(pltpu.VMEM((size, SMALL, 256), bf16))
    vmem = pl.BlockSpec(memory_space=pltpu.VMEM)
    smem = pl.BlockSpec(memory_space=pltpu.SMEM)
    grad, gup, gdown, gsmall = pl.pallas_call(
        functools.partial(body, tiles, phases),
        out_shape=[
            jax.ShapeDtypeStruct((SIDE * SIDE, 256), bf16),
            jax.ShapeDtypeStruct((256, 1024), bf16),
            jax.ShapeDtypeStruct((1024, 256), bf16),
            jax.ShapeDtypeStruct((SMALL, 256), f32),
        ],
        in_specs=[vmem] * 7 + [smem] * 2 + [vmem] * 5,
        out_specs=[vmem] * 4,
        scratch_shapes=scratch,
        compiler_params=pltpu.CompilerParams(
            collective_id=0, has_side_effects=True, vmem_limit_bytes=48 * 2**20
        ),
        cost_estimate=pl.CostEstimate(flops=10**9, bytes_accessed=8 * 2**20, transcendentals=2**18),
        name="block",
    )(
        fields.reshape(SIDE * SIDE, 256), upstream.reshape(SIDE * SIDE, 256),
        kernel.reshape(49, 256), gain.reshape(1, 256), w_up, w_down, scale.reshape(1, 256),
        spins, corner_counts, *tables(),
    )
    factor = 1.0 / math.sqrt(tiles * reps * SIDE * SIDE)
    return (
        grad.reshape(fields.shape),
        gsmall[:49].reshape(7, 7, 256) * factor,
        gsmall[49] * factor,
        gup.astype(f32) * factor,
        gdown.astype(f32) * factor,
        gsmall[50] * factor,
    )


def solution(mesh):
    spread = P("rep", "tile", None, None, None)
    return jax.shard_map(
        functools.partial(on_device, mesh.shape["tile"], mesh.shape["rep"]),
        mesh=mesh,
        in_specs=(spread, spread) + (P(),) * 7,
        out_specs=(spread,) + (P(),) * 5,
        check_vma=False,
    )
```

time: 307 us -> 58.6 us (0.19)
  waiting for transfers between devices: 131 us -> 0 us
  Pallas kernels: 0 us -> 43.4 us
  blocking collectives: 39.6 us -> 0 us
  local copies, waits for them, and re-layouts: 46 us -> 11.3 us
  other arithmetic: 34.9 us -> 2.73 us
  starting transfers between devices: 27.9 us -> 0 us
  between operations: 18.9 us -> 0.69 us
  matrix products: 5.9 us -> 0 us
    psum x1 -> x0, waiting for transfers between devices: 124 us -> none  [on_device(): lax.psum((g_kernel, g_gain, g_up, g_down, g_scale), ('tile', 'rep'))]
    pallas_call x0 -> x1, Pallas kernels: none -> 43.4 us  [on_device(): pl.pallas_call(functools.partial(body, tiles, phases), out_shape=[jax.Sha...]
    psum x1 -> x0, blocking collectives: 39.6 us -> none  [on_device(): lax.psum((g_kernel, g_gain, g_up, g_down, g_scale), ('tile', 'rep'))]
    ppermute x16 -> x0, starting transfers between devices: 27.8 us -> none  [shifted(): return lax.ppermute(block, axis, route)]
    scatter-add x51 -> x0, local copies, waits for them, and re-layouts: 23.2 us -> none  [the longest x43 21.9 us: block_grads(): grad_pad = grad_pad.at[:, row_off:row_off + side_len, col_off:col_off + s...]
    another operation x15 -> x0, other arithmetic: 18.8 us -> none
    ppermute x16 -> x0, waiting for transfers between devices: 7.36 us -> none  [shifted(): return lax.ppermute(block, axis, route)]
    scatter x8 -> x0, local copies, waits for them, and re-layouts: 6.38 us -> none  [the longest x4 5.68 us: assemble(): turned.at[..., :3, 3:-3, :].set(halo_cells[..., side_idx, ::-1, :, :])]
  transfers between devices with their start and end apart: 17 -> 0, of which waited for: 4 -> 0; matrix products, arithmetic and copies ran while one was open for 3% -> 0% of each run, Pallas kernels for 0% -> 0%
where the time goes in v1:
time: 58.6 us; the launch traced here: 58.1 us
  Pallas kernels  43.4 us (74%)
  local copies, waits for them, and re-layouts  11.3 us (19%)
  other arithmetic  2.73 us (5%)
  between operations  0.69 us (1%)
    pallas_call x1, Pallas kernels, on_device(): pl.pallas_call(functools.partial(body, tiles, phases), out_shape=[jax.Sha...  43.4 us
    unnamed x26, local copies, waits for them, and re-layouts  9.8 us

profile of v1, /device:TPU:1, one launch (start us, length us, event | category | flops | bytes accessed | tf_op | source)
XLA Modules:
  0.0 58.1 jit_solution(17245412174512965207)
XLA Ops:
  0.6 0.0 copy-start.2
  0.6 0.8 %copy.20.counts_ref = s32[16,4]{1,0:T(8,128)S(1)} copy(s32[16,4]{0,1:T(4,128)} %param.22) | data formatting | bytes 512 | tf_op args[8]
  1.4 0.0 copy-start.4
  1.4 0.0 copy-start.6
  1.4 0.9 %reshape.39.kern_ref = f32[49,256]{1,0:T(8,128)S(1)} reshape(f32[7,7,256]{2,1,0:T(8,128)} %param.16) | data formatting | bytes 100352 | tf_op jit(solution)/shard_map/reshape | solution.py:403
  2.3 0.0 copy-done.2
  2.3 0.0 copy-done.4
  2.3 0.0 copy-done.6
  2.3 0.0 copy-start
  2.3 1.0 %copy-done = bf16[256,1024]{1,0:T(8,128)(2,1)S(1)} copy-done((bf16[256,1024]{1,0:T(8,128)(2,1)S(1)}, bf16[256,1024]{1,0:T(8,128)(2,1)}, u32[]{:S(2)}) %copy-start) | copy-done | bytes 524312
  3.4 0.0 copy-start.1
  3.4 1.0 %copy-done.1 = bf16[1024,256]{1,0:T(8,128)(2,1)S(1)} copy-done((bf16[1024,256]{1,0:T(8,128)(2,1)S(1)}, bf16[1024,256]{1,0:T(8,128)(2,1)}, u32[]{:S(2)}) %copy-start.1) | copy-done | bytes 524312
  4.4 0.0 copy-start.3
  4.4 0.9 %copy-done.3 = bf16[1,1,16,16,256]{4,3,2,1,0:T(8,128)(2,1)S(1)} copy-done((bf16[1,1,16,16,256]{4,3,2,1,0:T(8,128)(2,1)S(1)}, bf16[1,1,16,16,256]{4,3,2,1,0:T(8,128)(2,1)}, u32[]{:S(2)}) %copy-start.3) | copy-done | bytes 131096
  5.3 0.0 copy-start.5
  5.3 0.7 %copy-done.5 = f32[256]{0:T(256)S(1)} copy-done((f32[256]{0:T(256)S(1)}, f32[256]{0:T(256)}, u32[]{:S(2)}) %copy-start.5) | copy-done | bytes 1048
  6.0 0.0 copy-start.7
  6.0 1.0 %copy-done.7 = bf16[256,528]{1,0:T(8,128)(2,1)S(1)} copy-done((bf16[256,528]{1,0:T(8,128)(2,1)S(1)}, bf16[256,528]{1,0:T(8,128)(2,1)}, u32[]{:S(2)}) %copy-start.7) | copy-done | bytes 270360
  7.0 0.0 copy-start.8
  7.0 1.0 %copy-done.8 = bf16[528,256]{1,0:T(8,128)(2,1)S(1)} copy-done((bf16[528,256]{1,0:T(8,128)(2,1)S(1)}, bf16[528,256]{1,0:T(8,128)(2,1)}, u32[]{:S(2)}) %copy-start.8) | copy-done | bytes 270360
  7.9 0.0 copy-start.9
  7.9 1.0 %copy-done.9 = bf16[528,256]{1,0:T(8,128)(2,1)S(1)} copy-done((bf16[528,256]{1,0:T(8,128)(2,1)S(1)}, bf16[528,256]{1,0:T(8,128)(2,1)}, u32[]{:S(2)}) %copy-start.9) | copy-done | bytes 270360
  8.9 0.0 copy-start.10
  8.9 0.9 %copy-done.10 = bf16[256,256]{1,0:T(8,128)(2,1)S(1)} copy-done((bf16[256,256]{1,0:T(8,128)(2,1)S(1)}, bf16[256,256]{1,0:T(8,128)(2,1)}, u32[]{:S(2)}) %copy-start.10) | copy-done | bytes 131096
  9.8 0.0 copy-start.11
  9.8 0.9 %copy-done.11 = bf16[256,256]{1,0:T(8,128)(2,1)S(1)} copy-done((bf16[256,256]{1,0:T(8,128)(2,1)S(1)}, bf16[256,256]{1,0:T(8,128)(2,1)}, u32[]{:S(2)}) %copy-start.11) | copy-done | bytes 131096
  10.7 43.4 %block.1 = (bf16[256,256]{1,0:T(8,128)(2,1)S(1)}, bf16[256,1024]{1,0:T(8,128)(2,1)S(1)}, bf16[1024,256]{1,0:T(8,128)(2,1)S(1)}, f32[64,256]{1,0:T(8,128)S(1)}) custom-call(bf16[256,256]{1,0:T(8,128)(2,1)S(1)} %bitcast.8, bf16[256,256]{1,0:T(8,128)(2,1)S(1)} %bitcast.9, f32[49,256]{1,0:T(8,128)S(1)} %reshape.39.kern_ref, f32[1,256]{1,0:T(1,128)S(1)} %bitcast.10, ...), custom_call_target="tpu_custom_call" | custom-call | flops 1000000000 | bytes 8388608 | tf_op jit(solution)/shard_map/block/pallas_call | solution.py:385
  54.1 0.6 slice_multiply_fusion.1
  54.7 0.6 %mul.35 = f32[7,7,256]{2,1,0:T(8,128)} reshape(f32[49,256]{1,0:T(8,128)S(1)} %slice_multiply_fusion) | data formatting | bytes 100352 | tf_op jit(solution)/shard_map/mul | solution.py:409
  55.3 1.1 %convert_multiply_fusion.1 = f32[256,1024]{1,0:T(8,128)} fusion(bf16[256,1024]{1,0:T(8,128)(2,1)S(1)} %get-tuple-element.12), kind=kLoop, calls=%fused_computation.1 | loop fusion | flops 524288 | bytes 1572864 | tf_op jit(solution)/shard_map/mul | solution.py:411
  56.4 1.1 %convert_multiply_fusion = f32[1024,256]{1,0:T(8,128)} fusion(bf16[1024,256]{1,0:T(8,128)(2,1)S(1)} %get-tuple-element.13), kind=kLoop, calls=%fused_computation | loop fusion | flops 524288 | bytes 1572864 | tf_op jit(solution)/shard_map/mul | solution.py:412
  57.5 0.7 %copy.22 = bf16[1,1,16,16,256]{4,3,2,1,0:T(8,128)(2,1)} copy(bf16[1,1,16,16,256]{4,3,2,1,0:T(8,128)(2,1)S(1)} %bitcast.7) | data formatting | bytes 262144
  (1 shorter events, 0.0 us)
Async XLA Ops:
  0.6 1.7 %copy-start.2 = (bf16[1,1,16,16,256]{4,3,2,1,0:T(8,128)(2,1)S(1)}, bf16[1,1,16,16,256]{4,3,2,1,0:T(8,128)(2,1)}, u32[]{:S(2)}) copy-start(bf16[1,1,16,16,256]{4,3,2,1,0:T(8,128)(2,1)} %param.14) | copy-start | bytes 393220
  1.4 0.9 %copy-start.4 = (f32[256]{0:T(256)S(1)}, f32[256]{0:T(256)}, u32[]{:S(2)}) copy-start(f32[256]{0:T(256)} %param.17) | copy-start | bytes 3076
  1.4 0.9 %copy-start.6 = (s32[16]{0:T(128)S(1)}, s32[16]{0:T(128)}, u32[]{:S(2)}) copy-start(s32[16]{0:T(128)} %spins_ref.1) | copy-start | bytes 196
  2.3 1.0 %copy-start = (bf16[256,1024]{1,0:T(8,128)(2,1)S(1)}, bf16[256,1024]{1,0:T(8,128)(2,1)}, u32[]{:S(2)}) copy-start(bf16[256,1024]{1,0:T(8,128)(2,1)} %wup_ref.1) | copy-start | bytes 1572868
  3.4 1.0 %copy-start.1 = (bf16[1024,256]{1,0:T(8,128)(2,1)S(1)}, bf16[1024,256]{1,0:T(8,128)(2,1)}, u32[]{:S(2)}) copy-start(bf16[1024,256]{1,0:T(8,128)(2,1)} %wdown_ref.1) | copy-start | bytes 1572868
  4.4 0.9 %copy-start.3 = (bf16[1,1,16,16,256]{4,3,2,1,0:T(8,128)(2,1)S(1)}, bf16[1,1,16,16,256]{4,3,2,1,0:T(8,128)(2,1)}, u32[]{:S(2)}) copy-start(bf16[1,1,16,16,256]{4,3,2,1,0:T(8,128)(2,1)} %param.15) | copy-start | bytes 393220
  5.3 0.7 %copy-start.5 = (f32[256]{0:T(256)S(1)}, f32[256]{0:T(256)}, u32[]{:S(2)}) copy-start(f32[256]{0:T(256)} %param.20) | copy-start | bytes 3076
  6.0 1.0 %copy-start.7 = (bf16[256,528]{1,0:T(8,128)(2,1)S(1)}, bf16[256,528]{1,0:T(8,128)(2,1)}, u32[]{:S(2)}) copy-start(bf16[256,528]{1,0:T(8,128)(2,1)} %constant.18.clone.paste_t_ref) | copy-start | bytes 811012
  7.0 1.0 %copy-start.8 = (bf16[528,256]{1,0:T(8,128)(2,1)S(1)}, bf16[528,256]{1,0:T(8,128)(2,1)}, u32[]{:S(2)}) copy-start(bf16[528,256]{1,0:T(8,128)(2,1)} %constant.19.clone.centre_ref) | copy-start | bytes 811012
  7.9 1.0 %copy-start.9 = (bf16[528,256]{1,0:T(8,128)(2,1)S(1)}, bf16[528,256]{1,0:T(8,128)(2,1)}, u32[]{:S(2)}) copy-start(bf16[528,256]{1,0:T(8,128)(2,1)} %constant.5.clone.paste_ref) | copy-start | bytes 811012
  8.9 0.9 %copy-start.10 = (bf16[256,256]{1,0:T(8,128)(2,1)S(1)}, bf16[256,256]{1,0:T(8,128)(2,1)}, u32[]{:S(2)}) copy-start(bf16[256,256]{1,0:T(8,128)(2,1)} %constant.8.clone.cut_t_ref) | copy-start | bytes 393220
  9.8 0.9 %copy-start.11 = (bf16[256,256]{1,0:T(8,128)(2,1)S(1)}, bf16[256,256]{1,0:T(8,128)(2,1)}, u32[]{:S(2)}) copy-start(bf16[256,256]{1,0:T(8,128)(2,1)} %constant.7.clone.cut_ref) | copy-start | bytes 393220

commit v2 on v1

--- a/solution.py
+++ b/solution.py
@@ -18,7 +18,16 @@
 PITCH = 24
 PIECE = 64
 SMALL = 64
-PARTS = 2
+PARTS = 4
+BACKWARDS = (1,)
+ARGS = (
+    "field", "up", "kern", "gain", "wup", "wdown", "scale", "spins", "counts",
+    "cut", "cut_t", "paste", "paste_t", "centre",
+)
+LOADS = (
+    "field", "cut", "spins", "up", "scale", "wdown", "centre", "counts", "paste", "kern",
+    "gain", "wup", "paste_t", "cut_t",
+)
 
 
 def tables():
@@ -44,7 +53,7 @@
     return [jnp.asarray(t, jnp.bfloat16) for t in (cut, cut.T, paste, paste.T, centre)]
 
 
-def plan(tiles, reps, rows):
+def plan(tiles, reps, rows, backwards=False):
     groups = []
     if reps > 1:
         groups.append(("rep", 1, reps))
@@ -53,6 +62,8 @@
         size = 4 if tiles // stride % 4 == 0 else 2
         groups.append(("tile", stride, size))
         stride *= size
+    if backwards:
+        groups = [g for g in groups if g[0] == "rep"] + [g for g in groups if g[0] != "rep"][::-1]
     phases = []
     for axis, stride, size in groups:
         scatter = rows % (16 * size) == 0
@@ -67,7 +78,27 @@
 
 
 def body(
-    tiles, phases,
+    tiles, plans,
+    *refs,
+):
+    sources, refs = refs[:14], refs[14:]
+    outputs, refs = refs[:4], refs[4:]
+    held, load_sem, refs = refs[:14], refs[14], refs[15:]
+    loads = {}
+    for name in LOADS:
+        slot = ARGS.index(name)
+        loads[name] = pltpu.make_async_copy(sources[slot], held[slot], load_sem.at[slot])
+        loads[name].start()
+
+    def need(*names):
+        for name in names:
+            loads[name].wait()
+
+    work(tiles, plans, need, *held, *outputs, *refs)
+
+
+def work(
+    tiles, plans, need,
     field_ref, up_ref, kern_ref, gain_ref, wup_ref, wdown_ref, scale_ref, spins_ref, counts_ref,
     cut_ref, cut_t_ref, paste_ref, paste_t_ref, centre_ref,
     grad_ref, gup_ref, gdown_ref, gsmall_ref,
@@ -75,10 +106,12 @@
     pad_ref, shift_ref, conv_ref, dact_ref, dcp_ref, dpad_ref, gbuf, agbuf, small_ref,
     send_sem, recv_sem, *bufs,
 ):
+    phases = plans[0]
     count = len(phases)
-    recv_bufs = bufs[:count]
-    red_bufs = bufs[count : 2 * count]
-    small_bufs = bufs[2 * count : 3 * count]
+    recv_bufs = [bufs[part * count : (part + 1) * count] for part in range(PARTS)]
+    bufs = bufs[PARTS * count :]
+    red_bufs = [bufs[part * count : (part + 1) * count] for part in range(PARTS)]
+    small_bufs = bufs[PARTS * count :]
     tile = lax.axis_index("tile")
     rep = lax.axis_index("rep")
     side = tiles // 2 ** ((tiles.bit_length() - 1) // 2)
@@ -87,13 +120,13 @@
     def across(step):
         return {"tile": lax.rem(tile + step + tiles, tiles)}
 
-    def place(phase):
+    def place(phase, phases=phases):
         axis, stride, size = phases[phase][:3]
         return rep if axis == "rep" else lax.rem(tile // stride, size)
 
-    def member(phase, ahead):
+    def member(phase, ahead, phases=phases):
         axis, stride, size = phases[phase][:3]
-        pos = place(phase)
+        pos = place(phase, phases)
         other = lax.rem(pos + ahead, size)
         if axis == "rep":
             return {"rep": other}, other
@@ -125,14 +158,13 @@
         started.append(copy)
         return copy
 
-    spin = spins_ref[tile]
     is_corner = lax.broadcasted_iota(jnp.int32, (PIECE, 256), 0) >= 48
 
     def masked(piece, edge):
-        keep = jnp.where(is_corner, counts_ref[tile, edge].astype(jnp.float32), 1.0)
+        keep = jnp.where(is_corner, keeps[edge : edge + 1, :], 1.0)
         return (piece.astype(jnp.float32) * keep).astype(jnp.bfloat16)
 
-    def trade(source, out, into):
+    def trade(source, out, into, spin):
         for grid in range(4):
             out[grid] = source[lax.rem(grid - spin + 4, 4)]
         copies = []
@@ -145,50 +177,52 @@
     flying = [None] * PARTS
     reached = [0] * PARTS
     offsets = []
-    offset = 0
-    for phase in range(count):
-        if phases[phase][3]:
-            offset = offset + place(phase) * phases[phase][5]
-        offsets.append(offset)
+    for ways in plans:
+        offset = 0
+        offsets.append([])
+        for phase in range(count):
+            if ways[phase][3]:
+                offset = offset + place(phase, ways) * ways[phase][5]
+            offsets[-1].append(offset)
 
     def source_of(part, phase):
-        return gbuf.at[part] if phase == 0 else red_bufs[phase - 1].at[part]
+        return gbuf.at[part] if phase == 0 else red_bufs[part][phase - 1]
 
     def begin(part):
-        phase = reached[part]
-        size, scatter, rows, out = phases[phase][2:]
+        phase, ways = reached[part], plans[part]
+        size, scatter, rows, out = ways[phase][2:]
         src = source_of(part, phase)
         copies = []
         if not scatter:
-            recv_bufs[phase][part, place(phase)] = src[...]
+            recv_bufs[part][phase][place(phase, ways)] = src[...]
         for ahead in range(1, size):
-            device, other = member(phase, ahead)
+            device, other = member(phase, ahead, ways)
             if scatter:
                 start = pl.multiple_of(other * out, 16)
-                copies.append(push(src.at[pl.ds(start, out)], recv_bufs[phase].at[part, ahead - 1], device))
+                copies.append(push(src.at[pl.ds(start, out)], recv_bufs[part][phase].at[ahead - 1], device))
             else:
-                copies.append(push(src, recv_bufs[phase].at[part, place(phase)], device))
+                copies.append(push(src, recv_bufs[part][phase].at[place(phase, ways)], device))
         flying[part] = copies
 
     def finish(part):
-        phase = reached[part]
-        size, scatter, rows, out = phases[phase][2:]
+        phase, ways = reached[part], plans[part]
+        size, scatter, rows, out = ways[phase][2:]
         src = source_of(part, phase)
         for copy in flying[part]:
             copy.wait_recv()
         if scatter:
-            total = src[pl.ds(pl.multiple_of(place(phase) * out, 16), out)].astype(jnp.float32)
+            total = src[pl.ds(pl.multiple_of(place(phase, ways) * out, 16), out)].astype(jnp.float32)
             for slot in range(size - 1):
-                total = total + recv_bufs[phase][part, slot].astype(jnp.float32)
+                total = total + recv_bufs[part][phase][slot].astype(jnp.float32)
         else:
-            total = recv_bufs[phase][part, 0].astype(jnp.float32)
+            total = recv_bufs[part][phase][0].astype(jnp.float32)
             for slot in range(1, size):
-                total = total + recv_bufs[phase][part, slot].astype(jnp.float32)
+                total = total + recv_bufs[part][phase][slot].astype(jnp.float32)
         reached[part] += 1
         if reached[part] < count:
-            red_bufs[phase][part] = total.astype(jnp.bfloat16)
+            red_bufs[part][phase][...] = total.astype(jnp.bfloat16)
         else:
-            agbuf[part, pl.ds(pl.multiple_of(offsets[-1], 16), out)] = total.astype(jnp.bfloat16)
+            agbuf[part, pl.ds(pl.multiple_of(offsets[part][-1], 16), out)] = total.astype(jnp.bfloat16)
 
     def advance(part):
         if reached[part] < count:
@@ -197,20 +231,27 @@
                 begin(part)
 
     def gather(part, phase):
-        size, scatter, rows, out = phases[phase][2:]
+        ways = plans[part]
+        size, scatter, rows, out = ways[phase][2:]
         if not scatter:
             return []
-        here = agbuf.at[part, pl.ds(pl.multiple_of(offsets[phase], 16), out)]
-        return [push(here, here, member(phase, ahead)[0]) for ahead in range(1, size)]
-
+        here = agbuf.at[part, pl.ds(pl.multiple_of(offsets[part][phase], 16), out)]
+        return [push(here, here, member(phase, ahead, ways)[0]) for ahead in range(1, size)]
+
+    need("field", "cut", "spins")
+    spin = spins_ref[tile]
     pieces[...] = dot(cut_ref[...], field_ref[...]).astype(jnp.bfloat16).reshape(4, PIECE, 256)
     pl.semaphore_wait(barrier, greeted)
-    copies = trade(pieces, sent, got)
+    copies = trade(pieces, sent, got, spin)
+    need("up", "scale", "wdown")
     upstream = up_ref[...].astype(jnp.float32)
     d_out = (upstream * scale_ref[...]).astype(jnp.bfloat16)
     for block in range(4):
         cols = pl.ds(block * 256, 256)
         dact_ref[:, cols] = dot(d_out, wdown_ref[cols, :], ((1,), (1,)))
+    need("centre", "counts", "paste", "kern", "gain", "wup", "paste_t", "cut_t")
+    mine = lax.broadcasted_iota(jnp.int32, (4, tiles), 1) == tile
+    keeps = jnp.sum(jnp.where(mine, counts_ref[...].astype(jnp.float32), 0.0), axis=1, keepdims=True)
     inner = dot(centre_ref[...], field_ref[...])
     dcp_ref[0:6] = jnp.zeros((6, SIDE, 256), jnp.float32)
     dcp_ref[WIDE : WIDE + 6] = jnp.zeros((6, SIDE, 256), jnp.float32)
@@ -228,7 +269,7 @@
         acc = [jnp.zeros((SIDE, 256), jnp.float32) for _ in range(4)]
         for col in range(7):
             for row in range(7):
-                tap = kern_ref[pl.ds(row * 7 + col, 1), :]
+                tap = kern_ref[row, pl.ds(col, 1), :]
                 for line in range(4):
                     acc[line] = acc[line] + shift_ref[col, group * 4 + line + row] * tap
         for line in range(4):
@@ -279,7 +320,7 @@
         for col in range(7):
             acc = [jnp.zeros((SIDE, 256), jnp.float32) for _ in range(2)]
             for row in range(7):
-                tap = kern_ref[pl.ds(row * 7 + col, 1), :]
+                tap = kern_ref[row, pl.ds(col, 1), :]
                 for line in range(2):
                     acc[line] = acc[line] + dcp_ref[group * 2 + line + 6 - row] * tap
             for line in range(2):
@@ -292,7 +333,7 @@
     back = dot(paste_t_ref[...], rounded).astype(jnp.bfloat16)
     for edge in range(4):
         pieces_b[edge] = masked(back[edge * PIECE : (edge + 1) * PIECE], edge)
-    copies = trade(pieces_b, sent_b, got_b)
+    copies = trade(pieces_b, sent_b, got_b, spin)
     for part in range(PARTS):
         advance(part)
 
@@ -352,14 +393,57 @@
         copy.wait_send()
 
 
+def finish_all(
+    factor, grad_ref, gup_ref, gdown_ref, gsmall_ref,
+    out_grad, out_kernel, out_gain, out_up, out_down, out_scale,
+    kernel_f, gain_f, scale_f, up_f, down_f, sem,
+):
+    copies = []
+
+    def write(src, dst):
+        copy = pltpu.make_async_copy(src, dst, sem.at[len(copies)])
+        copy.start()
+        copies.append(copy)
+
+    write(grad_ref, out_grad)
+    for block in range(4):
+        rows = pl.ds(block * 256, 256)
+        down_f[rows] = gdown_ref[rows, :].astype(jnp.float32) * factor
+        write(down_f.at[rows], out_down.at[rows])
+    for block in range(4):
+        rows = pl.ds(block * 64, 64)
+        up_f[rows] = gup_ref[rows, :].astype(jnp.float32) * factor
+        write(up_f.at[rows], out_up.at[rows])
+    small = gsmall_ref[...] * factor
+    for row in range(7):
+        kernel_f[row] = small[row * 7 : row * 7 + 7]
+    gain_f[...] = small[49:50]
+    scale_f[...] = small[50:51]
+    write(kernel_f, out_kernel)
+    write(gain_f, out_gain)
+    write(scale_f, out_scale)
+    for copy in copies:
+        copy.wait()
+
+
 def on_device(tiles, reps, fields, upstream, kernel, gain, w_up, w_down, scale, spins, corner_counts):
     rows = 2048 // PARTS
-    phases = plan(tiles, reps, rows)
+    plans = [plan(tiles, reps, rows, part in BACKWARDS) for part in range(PARTS)]
+    phases = plans[0]
     bf16, f32 = jnp.bfloat16, jnp.float32
     per_part = sum(size - 1 for _, _, size, _, _, _ in phases)
     sems = 16 + per_part * (2 * PARTS + 1)
     piece = pltpu.VMEM((4, PIECE, 256), bf16)
+    vector = pltpu.VMEM
     scratch = [
+        vector((SIDE * SIDE, 256), bf16), vector((SIDE * SIDE, 256), bf16),
+        vector((7, 7, 256), f32), vector((1, 256), f32),
+        vector((256, 1024), bf16), vector((1024, 256), bf16), vector((1, 256), f32),
+        pltpu.SMEM((tiles,), jnp.int32), vector((4, tiles), jnp.int32),
+        vector((4 * PIECE, SIDE * SIDE), bf16), vector((SIDE * SIDE, 4 * PIECE), bf16),
+        vector((WIDE * PITCH, 4 * PIECE), bf16), vector((4 * PIECE, WIDE * PITCH), bf16),
+        vector((WIDE * PITCH, SIDE * SIDE), bf16),
+        pltpu.SemaphoreType.DMA((14,)),
         piece, piece, piece, piece, piece, piece,
         pltpu.VMEM((4 * PIECE, 256), bf16),
         pltpu.VMEM((WIDE, PITCH, 256), f32),
@@ -374,43 +458,61 @@
         pltpu.SemaphoreType.DMA((sems,)),
         pltpu.SemaphoreType.DMA((sems,)),
     ]
-    for _, _, size, scatter, _, out in phases:
-        scratch.append(pltpu.VMEM((PARTS, size - 1 if scatter else size, out, 256), bf16))
-    for _, _, size, scatter, _, out in phases:
-        scratch.append(pltpu.VMEM((PARTS, out, 256), bf16))
+    for ways in plans:
+        for _, _, size, scatter, _, out in ways:
+            scratch.append(pltpu.VMEM((size - 1 if scatter else size, out, 256), bf16))
+    for ways in plans:
+        for _, _, _, _, _, out in ways:
+            scratch.append(pltpu.VMEM((out, 256), bf16))
     for _, _, size, _, _, _ in phases:
         scratch.append(pltpu.VMEM((size, SMALL, 256), bf16))
     vmem = pl.BlockSpec(memory_space=pltpu.VMEM)
-    smem = pl.BlockSpec(memory_space=pltpu.SMEM)
+    anywhere = pl.BlockSpec(memory_space=pltpu.HBM)
     grad, gup, gdown, gsmall = pl.pallas_call(
-        functools.partial(body, tiles, phases),
+        functools.partial(body, tiles, plans),
         out_shape=[
-            jax.ShapeDtypeStruct((SIDE * SIDE, 256), bf16),
-            jax.ShapeDtypeStruct((256, 1024), bf16),
-            jax.ShapeDtypeStruct((1024, 256), bf16),
-            jax.ShapeDtypeStruct((SMALL, 256), f32),
+            pltpu.VMEM((SIDE * SIDE, 256), bf16),
+            pltpu.VMEM((256, 1024), bf16),
+            pltpu.VMEM((1024, 256), bf16),
+            pltpu.VMEM((SMALL, 256), f32),
         ],
-        in_specs=[vmem] * 7 + [smem] * 2 + [vmem] * 5,
+        in_specs=[anywhere] * 14,
         out_specs=[vmem] * 4,
         scratch_shapes=scratch,
         compiler_params=pltpu.CompilerParams(
-            collective_id=0, has_side_effects=True, vmem_limit_bytes=48 * 2**20
+            collective_id=0, has_side_effects=True, vmem_limit_bytes=57 * 2**20
         ),
         cost_estimate=pl.CostEstimate(flops=10**9, bytes_accessed=8 * 2**20, transcendentals=2**18),
         name="block",
     )(
         fields.reshape(SIDE * SIDE, 256), upstream.reshape(SIDE * SIDE, 256),
-        kernel.reshape(49, 256), gain.reshape(1, 256), w_up, w_down, scale.reshape(1, 256),
-        spins, corner_counts, *tables(),
+        kernel, gain.reshape(1, 256), w_up, w_down, scale.reshape(1, 256),
+        spins, corner_counts.T, *tables(),
     )
     factor = 1.0 / math.sqrt(tiles * reps * SIDE * SIDE)
+    grad, kernel_grad, gain_grad, up_grad, down_grad, scale_grad = pl.pallas_call(
+        functools.partial(finish_all, factor),
+        out_shape=[
+            jax.ShapeDtypeStruct((SIDE * SIDE, 256), bf16),
+            jax.ShapeDtypeStruct((7, 7, 256), f32),
+            jax.ShapeDtypeStruct((1, 256), f32),
+            jax.ShapeDtypeStruct((256, 1024), f32),
+            jax.ShapeDtypeStruct((1024, 256), f32),
+            jax.ShapeDtypeStruct((1, 256), f32),
+        ],
+        in_specs=[vmem] * 4,
+        out_specs=[anywhere] * 6,
+        scratch_shapes=[
+            pltpu.VMEM((7, 7, 256), f32), pltpu.VMEM((1, 256), f32), pltpu.VMEM((1, 256), f32),
+            pltpu.VMEM((256, 1024), f32), pltpu.VMEM((1024, 256), f32),
+            pltpu.SemaphoreType.DMA((12,)),
+        ],
+        compiler_params=pltpu.CompilerParams(vmem_limit_bytes=16 * 2**20),
+        name="finish",
+    )(grad, gup, gdown, gsmall)
     return (
-        grad.reshape(fields.shape),
-        gsmall[:49].reshape(7, 7, 256) * factor,
-        gsmall[49] * factor,
-        gup.astype(f32) * factor,
-        gdown.astype(f32) * factor,
-        gsmall[50] * factor,
+        grad.reshape(fields.shape), kernel_grad, gain_grad.reshape(256),
+        up_grad, down_grad, scale_grad.reshape(256),
     )
 
 

time: 58.6 us -> 41.6 us (0.71)
  local copies, waits for them, and re-layouts: 11.3 us -> 0 us
  other arithmetic: 2.73 us -> 0 us
  Pallas kernels: 43.4 us -> 40.8 us
    unnamed x26 -> x0, local copies, waits for them, and re-layouts: 9.8 us -> none
    mul x4 -> x0, other arithmetic: 2.73 us -> none  [the longest x1 1.09 us: on_device(): gup.astype(f32) * factor]
    pallas_call x1 -> x2, Pallas kernels: 43.4 us -> 40.8 us  [the longest x1 39.4 us: on_device(): pl.pallas_call(functools.partial(body, tiles, plans), out_shape=[pltpu.VM...]
    reshape x1 -> x0, local copies, waits for them, and re-layouts: 0.85 us -> none  [on_device(): kernel.reshape(49, 256)]
    mul x1 -> x0, local copies, waits for them, and re-layouts: 0.63 us -> none  [on_device(): gsmall[:49].reshape(7, 7, 256) * factor]
where the time goes in v2:
time: 41.6 us; the launch traced here: 41.5 us
  Pallas kernels  40.8 us (98%)
  between operations  0.64 us (2%)
    pallas_call x1, Pallas kernels, on_device(): pl.pallas_call(functools.partial(body, tiles, plans), out_shape=[pltpu.VM...  39.4 us
    pallas_call x1, Pallas kernels, on_device(): pl.pallas_call(functools.partial(finish_all, factor), out_shape=[jax.Shap...  1.47 us

profile of v2, /device:TPU:1, one launch (start us, length us, event | category | flops | bytes accessed | tf_op | source)
XLA Modules:
  0.0 41.5 jit_solution(7480083621084341131)
XLA Ops:
  0.6 39.4 %block.1 = (bf16[256,256]{1,0:T(8,128)(2,1)S(1)}, bf16[256,1024]{1,0:T(8,128)(2,1)S(1)}, bf16[1024,256]{1,0:T(8,128)(2,1)S(1)}, f32[64,256]{1,0:T(8,128)S(1)}) custom-call(bf16[256,256]{1,0:T(8,128)(2,1)} %bitcast.8, bf16[256,256]{1,0:T(8,128)(2,1)} %bitcast.9, f32[7,7,256]{2,1,0:T(8,128)} %refs_2_.1, f32[1,256]{1,0:T(1,128)} %bitcast.12, ...), custom_call_target="tpu_custom_call" | custom-call | flops 1000000000 | bytes 8388608 | tf_op jit(solution)/shard_map/block/pallas_call | solution.py:471
  40.0 1.5 %finish.1 = (bf16[256,256]{1,0:T(8,128)(2,1)}, f32[7,7,256]{2,1,0:T(8,128)}, f32[1,256]{1,0:T(1,128)}, f32[256,1024]{1,0:T(8,128)}, f32[1024,256]{1,0:T(8,128)}, /*index=5*/f32[1,256]{1,0:T(1,128)}) custom-call(bf16[256,256]{1,0:T(8,128)(2,1)S(1)} %get-tuple-element.16.grad_ref, bf16[256,1024]{1,0:T(8,128)(2,1)S(1)} %get-tuple-element.17.gup_ref, ...), custom_call_target="tpu_custom_call" | custom-call | tf_op jit(solution)/shard_map/finish/pallas_call | solution.py:493

commit v3 on v2

--- a/solution.py
+++ b/solution.py
@@ -19,7 +19,7 @@
 PIECE = 64
 SMALL = 64
 PARTS = 4
-BACKWARDS = (1,)
+BACKWARDS = (0,)
 ARGS = (
     "field", "up", "kern", "gain", "wup", "wdown", "scale", "spins", "counts",
     "cut", "cut_t", "paste", "paste_t", "centre",
@@ -106,7 +106,7 @@
     pad_ref, shift_ref, conv_ref, dact_ref, dcp_ref, dpad_ref, gbuf, agbuf, small_ref,
     send_sem, recv_sem, *bufs,
 ):
-    phases = plans[0]
+    phases = plans[-1]
     count = len(phases)
     recv_bufs = [bufs[part * count : (part + 1) * count] for part in range(PARTS)]
     bufs = bufs[PARTS * count :]
@@ -429,7 +429,7 @@
 def on_device(tiles, reps, fields, upstream, kernel, gain, w_up, w_down, scale, spins, corner_counts):
     rows = 2048 // PARTS
     plans = [plan(tiles, reps, rows, part in BACKWARDS) for part in range(PARTS)]
-    phases = plans[0]
+    phases = plans[-1]
     bf16, f32 = jnp.bfloat16, jnp.float32
     per_part = sum(size - 1 for _, _, size, _, _, _ in phases)
     sems = 16 + per_part * (2 * PARTS + 1)

time: 41.6 us -> 42.1 us (1.012)
  Pallas kernels: 40.8 us -> 41.4 us
    pallas_call x1, Pallas kernels: 39.4 us -> 39.9 us  [on_device(): pl.pallas_call(functools.partial(body, tiles, plans), out_shape=[pltpu.VM...]
where the time goes in v3:
time: 42.1 us; the launch traced here: 42 us
  Pallas kernels  41.4 us (98%)
  between operations  0.64 us (2%)
    pallas_call x1, Pallas kernels, on_device(): pl.pallas_call(functools.partial(body, tiles, plans), out_shape=[pltpu.VM...  39.9 us
    pallas_call x1, Pallas kernels, on_device(): pl.pallas_call(functools.partial(finish_all, factor), out_shape=[jax.Shap...  1.47 us

profile of v3, /device:TPU:1, one launch (start us, length us, event | category | flops | bytes accessed | tf_op | source)
XLA Modules:
  0.0 42.0 jit_solution(17051928737889695325)
XLA Ops:
  0.6 39.9 %block.1 = (bf16[256,256]{1,0:T(8,128)(2,1)S(1)}, bf16[256,1024]{1,0:T(8,128)(2,1)S(1)}, bf16[1024,256]{1,0:T(8,128)(2,1)S(1)}, f32[64,256]{1,0:T(8,128)S(1)}) custom-call(bf16[256,256]{1,0:T(8,128)(2,1)} %bitcast.8, bf16[256,256]{1,0:T(8,128)(2,1)} %bitcast.9, f32[7,7,256]{2,1,0:T(8,128)} %refs_2_.1, f32[1,256]{1,0:T(1,128)} %bitcast.12, ...), custom_call_target="tpu_custom_call" | custom-call | flops 1000000000 | bytes 8388608 | tf_op jit(solution)/shard_map/block/pallas_call | solution.py:471
  40.5 1.5 %finish.1 = (bf16[256,256]{1,0:T(8,128)(2,1)}, f32[7,7,256]{2,1,0:T(8,128)}, f32[1,256]{1,0:T(1,128)}, f32[256,1024]{1,0:T(8,128)}, f32[1024,256]{1,0:T(8,128)}, /*index=5*/f32[1,256]{1,0:T(1,128)}) custom-call(bf16[256,256]{1,0:T(8,128)(2,1)S(1)} %get-tuple-element.16.grad_ref, bf16[256,1024]{1,0:T(8,128)(2,1)S(1)} %get-tuple-element.17.gup_ref, ...), custom_call_target="tpu_custom_call" | custom-call | tf_op jit(solution)/shard_map/finish/pallas_call | solution.py:493
